TPU v7x, 256 devices: a whole 4x4x8 slice. The times are simulated.
256 devices in a mesh: row: 8 (over x_lo, y), col: 32 (over z, x_hi, core).
Axes of the slice: x: 4 (x_hi: 2, x_lo: 2; x = x_hi * 2 + x_lo), y: 4, z: 8, core: 2. Of those that a mesh axis runs over, the one named last changes fastest.
Arguments:
- features: float32 [32, 8, 128, 512], P('col', 'row'), may hold values from -6 to 6
- adjacency: bfloat16 [32, 8, 32, 8, 128, 128], P(None, 'row', 'col'), may hold values from -0.0625 to 0.0625
- tile_mask: int32 [32, 8, 32, 8], P(None, 'row', 'col'), may hold values from 0 to 1, as said below
- projection: float32 [1, 512, 512], replicated, may hold values from -0.25 to 0.25
- row_gain: float32 [1, 512], replicated, may hold values from 0.5 to 1.5
Outputs:
- propagated: float32 [32, 8, 128, 512], P('col', 'row')
Inputs may be any that keep to these rules, and one draw needn't show every extreme that they name: `tile_mask`: 1 marks a present tile; every tile with k * 8 + r = c * 8 + m is present, and so is every tile whose two block numbers k * 8 + r and c * 8 + m differ by exactly 128; every other tile whose two block numbers differ by more than 102 is absent.
All inputs are finite; a program needn't handle non-finite values.
Results may differ from a plain program's by a relative error of at most 0.0021.
Values may be sent and summed in bfloat16 or wider, within the bound.
A program may use at most 128 MiB of HBM per device.

v0:
```python
import jax
import jax.numpy as jnp
from jax import lax
from jax.sharding import PartitionSpec as P


def mask_tiles(adjacency, tile_mask):
    present = tile_mask[:, 0, 0].astype(jnp.bfloat16)
    return adjacency[:, 0, 0] * present[:, :, None, None]


def shards(features, adjacency, tile_mask, projection, row_gain):
    masked = mask_tiles(adjacency, tile_mask)
    members = masked.shape[1]
    tile = masked.shape[2]
    width = features.shape[-1]
    current = features[0, 0]
    half = current.astype(jnp.bfloat16)
    chosen = masked
    shaped = lax.all_gather(half, "col", axis=0, tiled=True).reshape(-1, tile, width)
    backward = jnp.einsum("kmab,kaf->mbf", chosen, shaped, preferred_element_type=jnp.float32)
    totals = lax.psum(backward, "row")
    backward_sum = lax.dynamic_index_in_dim(totals, lax.axis_index("row"), 0, keepdims=False)
    gathered = lax.all_gather(half, "row", axis=0, tiled=True)
    column_half = gathered.reshape(members, tile, width)
    chosen = masked
    term = jnp.einsum("kmab,mbf->kaf", chosen, column_half, preferred_element_type=jnp.float32)
    forward_sum = lax.psum_scatter(
        term.reshape(lax.axis_size("col") * tile, width), "col", scatter_dimension=0, tiled=True
    )
    summed = forward_sum + backward_sum
    mixed = jnp.dot(
        summed, projection[0], precision=lax.Precision.HIGHEST, preferred_element_type=jnp.float32
    )
    lifted = current + jax.nn.relu(mixed)
    scale = lax.rsqrt(jnp.mean(lifted * lifted, axis=-1, keepdims=True) + 1e-06)
    current = lifted * scale * row_gain[0]
    return current[None, None]


def solution(mesh):
    return jax.shard_map(
        shards,
        mesh=mesh,
        in_specs=(
            P("col", "row", None, None),
            P(None, "row", "col", None, None, None),
            P(None, "row", "col", None),
            P(),
            P(),
        ),
        out_specs=P("col", "row", None, None),
        check_vma=False,
    )
```

profile of v0, /device:TPU:1, one launch (start us, length us, event | category | flops | bytes accessed | tf_op | source)
XLA Modules:
  0.0 393.0 jit_solution(5485793676232646158)
XLA Ops:
  6.5 0.0 copy-start
  6.5 0.0 all-gather.5.cloned.1.call-start
  6.5 1.7 bitcast_convert_fusion
  8.3 0.0 all-gather.5.cloned.1.call-update
  8.3 0.0 all-gather.3.cloned.1.call-start
  8.3 0.7 all-gather.3.cloned.1.call-update
  9.0 0.0 all-reduce.2.cloned.1.call-start
  9.1 0.7 convert_bitcast_fusion
  9.8 0.1 copy.9
  9.9 11.5 %bitcast_multiply_fusion = bf16[32,8,128,128]{3,1,2,0:T(8,128)(2,1)} fusion(bf16[32,1,1,8,128,128]{5,4,3,2,1,0:T(8,128)(2,1)} %param.6, bf16[32,8]{1,0:T(8,128)(2,1)S(1)} %copy.9), kind=kLoop, calls=%fused_computation | loop fusion | flops 4194304 | bytes 16777728 | tf_op jit(solution)/shard_map/mul | solution.py:9
  21.3 79.9 %all-gather.5.cloned.1.call-done = bf16[4096,512]{1,0:T(8,128)(2,1)} async-done(((bf16[128,512]{1,0:T(8,128)(2,1)}), bf16[4096,512]{1,0:T(8,128)(2,1)}) %all-gather.5.cloned.1.call-update) | async-done | bytes 4194320 | tf_op jit(solution)/shard_map/all_gather | solution.py:20
  101.2 10.4 %fusion.7 = f32[8,128,512]{2,1,0:T(8,128)} fusion(bf16[32,128,512,1]{2,1,0,3:T(8,128)(2,1)} %bitcast.36, bf16[32,8,128,128]{3,1,2,0:T(8,128)(2,1)} %bitcast_multiply_fusion), kind=kOutput, calls=%fused_computation.6 | convolution fusion | flops 4294967296 | bytes 14680064 | tf_op jit(solution)/shard_map/kmab,kaf->mbf/dot_general | solution.py:21
  111.6 0.0 all-reduce.2.cloned.1.call-update
  111.6 0.2 reduce-scatter.2.cloned.1.call-start
  111.8 24.0 %all-gather.3.cloned.1.call-done = bf16[1024,512]{1,0:T(8,128)(2,1)} async-done(((bf16[128,512]{1,0:T(8,128)(2,1)}), bf16[1024,512]{1,0:T(8,128)(2,1)}) %all-gather.3.cloned.1.call-update) | async-done | bytes 1048592 | tf_op jit(solution)/shard_map/all_gather | solution.py:24
  135.8 9.1 %fusion.4 = f32[4096,512]{1,0:T(8,128)} fusion(bf16[8,128,512]{2,1,0:T(8,128)(2,1)} %bitcast.37, bf16[4096,128,8]{1,2,0:T(8,128)(2,1)} %bitcast.34), kind=kOutput, calls=%fused_computation.5 | convolution fusion | flops 4294967296 | bytes 17825792 | tf_op jit(solution)/shard_map/kmab,mbf->kaf/dot_general | solution.py:27
  145.0 0.0 reduce-scatter.2.cloned.1.call-update
  145.0 81.0 %all-reduce.2.cloned.1.call-done = f32[8,128,512]{2,1,0:T(8,128)} async-done(((f32[8,128,512]{2,1,0:T(8,128)}), f32[8,128,512]{2,1,0:T(8,128)}) %all-reduce.2.cloned.1.call-update) | async-done | bytes 2097168 | tf_op jit(solution)/shard_map/psum | solution.py:22
  226.0 157.8 %reduce-scatter.2.cloned.1.call-done = f32[128,512]{1,0:T(8,128)} async-done(((f32[4096,512]{1,0:T(8,128)}), f32[128,512]{1,0:T(8,128)}) %reduce-scatter.2.cloned.1.call-update) | async-done | bytes 262160 | tf_op jit(solution)/shard_map/reduce_scatter | solution.py:28
  383.8 0.0 copy-done
  383.8 0.0 copy-done.1
  383.8 1.8 multiply_reduce_fusion
  385.6 0.0 copy-done.2
  385.6 0.8 multiply_bitcast_fusion
  (3 shorter events, 0.0 us)
Async XLA Ops:
  6.5 377.2 %copy-start = (f32[1,512,512]{2,1,0:T(8,128)S(1)}, f32[1,512,512]{2,1,0:T(8,128)}, u32[]{:S(2)}) copy-start(f32[1,512,512]{2,1,0:T(8,128)} %param.8) | copy-start | bytes 3145732
  6.5 94.7 %all-gather.5.cloned.1.call-start = ((), (), s32[]{:S(2)}) async-start(), calls=%async_computation.3 | async-start | bytes 4325376 | tf_op jit(solution)/shard_map/all_gather | solution.py:20
  8.3 127.6 %all-gather.3.cloned.1.call-start = ((), (), s32[]{:S(2)}) async-start(), calls=%async_computation.1 | async-start | bytes 1179648 | tf_op jit(solution)/shard_map/all_gather | solution.py:24
  9.0 217.0 %all-reduce.2.cloned.1.call-start = ((), (), s32[]{:S(2)}) async-start(), calls=%async_computation.4 | async-start | bytes 4194304 | tf_op jit(solution)/shard_map/psum | solution.py:22
  111.6 272.2 %reduce-scatter.2.cloned.1.call-start = ((), (), s32[]{:S(2)}) async-start(), calls=%async_computation.2 | async-start | bytes 8650752 | tf_op jit(solution)/shard_map/reduce_scatter | solution.py:28
  145.0 238.8 %copy-start.1 = (f32[1,1,128,512]{3,2,1,0:T(8,128)S(1)}, f32[1,1,128,512]{3,2,1,0:T(8,128)}, u32[]{:S(2)}) copy-start(f32[1,1,128,512]{3,2,1,0:T(8,128)} %param.5) | copy-start | bytes 786436
  145.0 240.6 %copy-start.2 = (f32[1,512]{1,0:T(1,128)S(1)}, f32[1,512]{1,0:T(1,128)}, u32[]{:S(2)}) copy-start(f32[1,512]{1,0:T(1,128)} %param.9) | copy-start | bytes 6148
Sparse Core Ops, SparseCore 0:
  10.1 91.0 all-gather.4
  103.0 32.8 all-gather.2
  138.5 87.4 all-reduce.1
  230.3 153.4 reduce-scatter.1
where the time goes:
time: 397 us; the launch traced here: 393 us
  waiting for transfers between devices  343 us (86%)
  matrix products  21.4 us (5%)
  other arithmetic  14.7 us (4%)
  between operations  13.2 us (3%)
    reduce_scatter x1, waiting for transfers between devices, shards(): lax.psum_scatter(term.reshape(lax.axis_size('col') * tile, width), 'col',...  158 us
    psum x1, waiting for transfers between devices, shards(): totals = lax.psum(backward, 'row')  81 us
    all_gather x1, waiting for transfers between devices, shards(): lax.all_gather(half, 'col', axis=0, tiled=True).reshape(-1, tile, width)  79.9 us
    all_gather x1, waiting for transfers between devices, shards(): gathered = lax.all_gather(half, 'row', axis=0, tiled=True)  24 us
    mul x1, other arithmetic, mask_tiles(): return adjacency[:, 0, 0] * present[:, :, None, None]  11.5 us
    dot_general x1, matrix products, shards(): jnp.einsum('kmab,kaf->mbf', chosen, shaped, preferred_element_type=jnp.fl...  10.4 us
    dot_general x1, matrix products, shards(): jnp.einsum('kmab,mbf->kaf', chosen, column_half, preferred_element_type=j...  9.14 us
  transfers between devices with their start and end apart: 4, of which 4 were waited for; matrix products, arithmetic and copies ran while one was open for 8% of the time, Pallas kernels for 0%

commit v1 on v0

v1 whole, which is shorter than its diff:
```python
import functools

import jax
import jax.numpy as jnp
from jax import lax
from jax.experimental import pallas as pl
from jax.experimental.pallas import tpu as pltpu
from jax.sharding import PartitionSpec as P

MESH = pl.DeviceIdType.MESH
TILE, F, NK, NM, NZ = 128, 512, 32, 8, 8


def kernel(x_ref, a_hbm, mask_ref, p_ref, g_ref, o_ref,
           am, nat, ht, keep, snd, sib, cs, cr, hs, hr, bs, br,
           a_sem, row_s, row_r, agz_s, agz_r, hp_s, hp_r, sh_s, sh_r,
           dd_s, dd_r, rsz_s, rsz_r, hx_s, hx_r, br_s, br_r):
    r = lax.axis_index("row")
    c = lax.axis_index("col")
    z = c // 4
    h = (c // 2) % 2
    q = c % 2
    sibling = (r, c + 1 - 2 * q)
    hpartner = (r, c + 2 - 4 * h)
    zdev = ((r, (c + 4) % NK), (r, (c + 28) % NK))

    def plane(d):
        return (z + d + 16) % NZ

    def half_of(hh):
        return h if hh == 1 else 1 - h

    def block(d, hh, qq):
        return 4 * plane(d) + 2 * half_of(hh) + qq

    sends = []

    def remote(src, dst, ssem, rsem, dev):
        return pltpu.make_async_remote_copy(
            src_ref=src, dst_ref=dst, send_sem=ssem, recv_sem=rsem,
            device_id=dev, device_id_type=MESH)

    def start(copy):
        copy.start()
        sends.append(copy)

    for m in range(NM):
        pltpu.make_async_copy(a_hbm.at[:, m], am.at[m], a_sem.at[m]).start()

    barrier = pltpu.get_barrier_semaphore()
    peers = [((r + j) % 8, c) for j in range(1, 8)] + [sibling, hpartner, zdev[0], zdev[1]]
    for dev in peers:
        pl.semaphore_signal(barrier, inc=1, device_id=dev, device_id_type=MESH)

    x = x_ref[...]
    nat[r] = x.astype(jnp.bfloat16)
    ht[c] = x.T.astype(jnp.bfloat16)
    pl.semaphore_wait(barrier, len(peers))

    def ag_ref(dirn, s, hh, sending):
        d = (1 - s if sending else -s) if dirn == 0 else (s - 1 if sending else s)
        ref = ht.at[block(d, hh, q)]
        if s == 4:
            ref = ref.at[pl.ds(256 * dirn, 256)]
        return ref

    def ag_send(dirn, s, hh):
        ref = ag_ref(dirn, s, hh, True)
        start(remote(ref, ref, agz_s.at[dirn, s - 1, hh], agz_r.at[dirn, s - 1, hh], zdev[dirn]))

    def ag_wait(dirn, s, hh):
        ref = ag_ref(dirn, s, hh, False)
        remote(ref, ref, agz_s.at[dirn, s - 1, hh], agz_r.at[dirn, s - 1, hh], zdev[dirn]).wait_recv()

    def share(d, hh):
        ref = ht.at[block(d, hh, q)]
        start(remote(ref, ref, sh_s.at[d, hh], sh_r.at[d, hh], sibling))

    def share_wait(d, hh):
        ref = ht.at[block(d, hh, 1 - q)]
        remote(ref, ref, sh_s.at[d, hh], sh_r.at[d, hh], sibling).wait_recv()

    def ag_step(s, hh):
        for dirn in range(2):
            ag_wait(dirn, s, hh)
            if s < 4:
                ag_send(dirn, s + 1, hh)
        if s < 4:
            share(8 - s, hh)
            share(s, hh)
        else:
            share(4, hh)

    ag_send(0, 1, 1)
    ag_send(1, 1, 1)
    own = ht.at[c]
    start(remote(own, own, hp_s, hp_r, hpartner))
    mine = nat.at[r]
    for j in range(1, 8):
        start(remote(mine, mine, row_s.at[j], row_r.at[j], ((r + j) % 8, c)))
    share(0, 1)

    def mask_tiles(m):
        pltpu.make_async_copy(a_hbm.at[:, m], am.at[m], a_sem.at[m]).wait()

        def body(k, carry):
            level = jnp.full((TILE, TILE), mask_ref[k, m].astype(jnp.float32))
            am[m, k] = am[m, k] * level.astype(jnp.bfloat16)
            return carry
        lax.fori_loop(0, NK, body, 0)

    for m in range(4):
        mask_tiles(m)
    other = ht.at[c + 2 - 4 * h]
    remote(other, other, hp_s, hp_r, hpartner).wait_recv()
    ag_send(0, 1, 0)
    ag_send(1, 1, 0)
    share(0, 0)
    for m in range(4, NM):
        mask_tiles(m)
    ag_step(1, 1)
    ag_step(1, 0)
    ag_step(2, 1)

    for j in range(1, 8):
        ref = nat.at[(r + 8 - j) % 8]
        remote(ref, ref, row_s.at[j], row_r.at[j], ((r + j) % 8, c)).wait_recv()

    def rows_of(k):
        return jnp.concatenate([am[m, k] for m in range(NM)], axis=1)

    def product(ds, qq):
        lhs = jnp.concatenate([rows_of(block(d, hh, qq)) for d in ds for hh in range(2)], axis=0)
        out = jnp.dot(lhs, nat[...].reshape(NM * TILE, F), preferred_element_type=jnp.float32)
        return out.reshape(len(ds), 2, TILE, F)

    def dd(d):
        return remote(snd.at[d], sib.at[d], dd_s.at[d], dd_r.at[d], sibling)

    def forward(ds):
        out = product(ds, 1 - q)
        for i, d in enumerate(ds):
            snd[d] = out[i]
            start(dd(d))
        out = product(ds, q)
        for i, d in enumerate(ds):
            keep[d] = out[i]

    def rsz(dirn, s, hh):
        src, dst = cs.at[dirn, s - 1, hh], cr.at[dirn, s - 1, hh]
        if s == 1:
            part = pl.ds(64 * dirn, 64)
            src, dst = src.at[part], dst.at[part]
        return remote(src, dst, rsz_s.at[dirn, s - 1, hh], rsz_r.at[dirn, s - 1, hh], zdev[dirn])

    def rs_step(s, hh):
        for dirn in range(2):
            d = 5 - s if dirn == 0 else 3 + s
            if hh == 0 and (s > 1 or dirn == 0):
                dd(d).wait_recv()
            lo = 64 * dirn
            if s > 1:
                rsz(dirn, s - 1, hh).wait_recv()
            if s == 1:
                part = slice(lo, lo + 64)
                cs[dirn, 0, hh, part] = (keep[d, hh, part] + sib[d, hh, part]).astype(jnp.bfloat16)
            elif s == 2:
                part = slice(lo, lo + 64)
                rest = slice(64 - lo, 128 - lo)
                cs[dirn, 1, hh, part] = (keep[d, hh, part] + sib[d, hh, part]
                                         + cr[dirn, 0, hh, part].astype(jnp.float32)).astype(jnp.bfloat16)
                cs[dirn, 1, hh, rest] = (keep[d, hh, rest] + sib[d, hh, rest]).astype(jnp.bfloat16)
            else:
                cs[dirn, s - 1, hh] = (keep[d, hh] + sib[d, hh]
                                       + cr[dirn, s - 2, hh].astype(jnp.float32)).astype(jnp.bfloat16)
            start(rsz(dirn, s, hh))

    def rs_total(hh):
        if hh == 0:
            dd(0).wait_recv()
        for dirn in range(2):
            rsz(dirn, 4, hh).wait_recv()
        return (keep[0, hh] + sib[0, hh] + cr[0, 3, hh].astype(jnp.float32)
                + cr[1, 3, hh].astype(jnp.float32))

    def brow(j):
        return remote(bs.at[j], br.at[j], br_s.at[j], br_r.at[j], ((r + j) % 8, c))

    def backward(ja, jb):
        ma, mb = (r + ja) % 8, (r + jb) % 8
        total = None
        for k0 in range(0, NK, 8):
            lhs = jnp.concatenate([ht[k] for k in range(k0, k0 + 8)], axis=1)
            rhs = jnp.concatenate(
                [am[mm, k0:k0 + 8].reshape(8 * TILE, TILE) for mm in (ma, mb)], axis=1)
            term = jnp.dot(lhs, rhs, preferred_element_type=jnp.float32)
            total = term if total is None else total + term
        for i, j in enumerate((ja, jb)):
            bs[j] = total[:, TILE * i:TILE * (i + 1)].astype(jnp.bfloat16)
            if j:
                start(brow(j))

    forward((4, 0))
    ag_step(2, 0)
    forward((3, 5))
    rs_step(1, 0)
    rs_step(1, 1)
    ag_step(3, 1)
    forward((2, 6))
    rs_step(2, 0)
    ag_step(3, 0)
    rs_step(2, 1)
    forward((1, 7))
    ag_step(4, 1)
    ag_step(4, 0)
    rs_step(3, 0)
    rs_step(3, 1)
    for d in range(8):
        for hh in (1, 0):
            share_wait(d, hh)
    backward(1, 2)
    backward(3, 4)
    rs_step(4, 0)
    rs_step(4, 1)
    backward(5, 6)
    backward(7, 0)

    hs[...] = rs_total(0)
    cross = remote(hs, hr, hx_s, hx_r, hpartner)
    start(cross)
    back = bs[0].astype(jnp.float32)
    for j in range(1, 8):
        brow(j).wait_recv()
        back = back + br[j].astype(jnp.float32)
    summed = rs_total(1) + back.T
    cross.wait_recv()
    summed = summed + hr[...]
    mixed = jnp.dot(summed, p_ref[...], precision=lax.Precision.HIGHEST,
                    preferred_element_type=jnp.float32)
    lifted = x_ref[...] + jnp.maximum(mixed, 0.0)
    scale = lax.rsqrt(jnp.mean(lifted * lifted, axis=-1, keepdims=True) + 1e-06)
    o_ref[...] = lifted * scale * g_ref[...]
    for copy in sends:
        copy.wait_send()


def shards(features, adjacency, tile_mask, projection, row_gain):
    vm = pl.BlockSpec(memory_space=pltpu.VMEM)
    bf, f32 = jnp.bfloat16, jnp.float32
    dma = pltpu.SemaphoreType.DMA
    out = pl.pallas_call(
        kernel,
        out_shape=jax.ShapeDtypeStruct((TILE, F), f32),
        in_specs=[vm, pl.BlockSpec(memory_space=pl.ANY),
                  pl.BlockSpec(memory_space=pltpu.SMEM), vm, vm],
        out_specs=vm,
        scratch_shapes=[
            pltpu.VMEM((NM, NK, TILE, TILE), bf),
            pltpu.VMEM((8, TILE, F), bf),
            pltpu.VMEM((NK, F, TILE), bf),
            pltpu.VMEM((8, 2, TILE, F), f32),
            pltpu.VMEM((8, 2, TILE, F), f32),
            pltpu.VMEM((8, 2, TILE, F), f32),
            pltpu.VMEM((2, 4, 2, TILE, F), bf),
            pltpu.VMEM((2, 4, 2, TILE, F), bf),
            pltpu.VMEM((TILE, F), f32),
            pltpu.VMEM((TILE, F), f32),
            pltpu.VMEM((8, F, TILE), bf),
            pltpu.VMEM((8, F, TILE), bf),
            dma((NM,)), dma((8,)), dma((8,)), dma((2, 4, 2)), dma((2, 4, 2)), dma, dma,
            dma((8, 2)), dma((8, 2)), dma((8,)), dma((8,)), dma((2, 4, 2)), dma((2, 4, 2)),
            dma, dma, dma((8,)), dma((8,)),
        ],
        compiler_params=pltpu.CompilerParams(
            collective_id=0, has_side_effects=True, vmem_limit_bytes=56 * 2**20),
        cost_estimate=pl.CostEstimate(
            flops=4 * 32 * 1024 * 128 * 512, bytes_accessed=9 * 2**20, transcendentals=128),
    )(features[0, 0], adjacency[:, 0, 0], tile_mask[:, 0, 0], projection[0], row_gain)
    return out[None, None]


def solution(mesh):
    return jax.shard_map(
        shards,
        mesh=mesh,
        in_specs=(
            P("col", "row", None, None),
            P(None, "row", "col", None, None, None),
            P(None, "row", "col", None),
            P(),
            P(),
        ),
        out_specs=P("col", "row", None, None),
        check_vma=False,
    )
```

time: 397 us -> 72.8 us (0.18)
  waiting for transfers between devices: 343 us -> 0 us
  Pallas kernels: 0 us -> 69.6 us
  matrix products: 21.4 us -> 0 us
  other arithmetic: 14.7 us -> 0 us
  between operations: 13.2 us -> 0.01 us
    reduce_scatter x1 -> x0, waiting for transfers between devices: 158 us -> none  [shards(): lax.psum_scatter(term.reshape(lax.axis_size('col') * tile, width), 'col',...]
    all_gather x2 -> x0, waiting for transfers between devices: 104 us -> none  [the longest x1 79.9 us: shards(): lax.all_gather(half, 'col', axis=0, tiled=True).reshape(-1, tile, width)]
    psum x1 -> x0, waiting for transfers between devices: 81 us -> none  [shards(): totals = lax.psum(backward, 'row')]
    pallas_call x0 -> x1, Pallas kernels: none -> 69.6 us  [shards(): pl.pallas_call(kernel, out_shape=jax.ShapeDtypeStruct((TILE, F), f32), in...]
    dot_general x3 -> x0, matrix products: 21.4 us -> none  [the longest x1 10.4 us: shards(): jnp.einsum('kmab,kaf->mbf', chosen, shaped, preferred_element_type=jnp.fl...]
    mul x1 -> x0, other arithmetic: 11.5 us -> none  [mask_tiles(): return adjacency[:, 0, 0] * present[:, :, None, None]]
  transfers between devices with their start and end apart: 4 -> 0, of which waited for: 4 -> 0; matrix products, arithmetic and copies ran while one was open for 8% -> 0% of each run, Pallas kernels for 0% -> 0%
where the time goes in v1:
time: 72.8 us; the launch traced here: 72.6 us
  Pallas kernels  69.6 us (96%)
  local copies, waits for them, and re-layouts  3.04 us (4%)
    pallas_call x1, Pallas kernels, shards(): pl.pallas_call(kernel, out_shape=jax.ShapeDtypeStruct((TILE, F), f32), in...  69.6 us
    unnamed x2, local copies, waits for them, and re-layouts  3.04 us

profile of v1, /device:TPU:1, one launch (start us, length us, event | category | flops | bytes accessed | tf_op | source)
XLA Modules:
  0.0 72.6 jit_solution(17206489195260313885)
XLA Ops:
  0.0 1.4 %copy.6 = s32[32,1,1,8]{3,0,2,1:T(8,128)} copy(s32[32,1,1,8]{0,3,2,1:T(8,128)} %param.7) | data formatting | bytes 2048 | tf_op args[2]
  1.4 69.6 %shard_map.55 = f32[128,512]{1,0:T(8,128)} custom-call(f32[128,512]{1,0:T(8,128)} %bitcast.9, bf16[32,8,128,128]{3,2,1,0:T(8,128)(2,1)} %bitcast.7, s32[32,8]{1,0:T(8,128)} %bitcast.6, f32[512,512]{1,0:T(8,128)} %bitcast.8, f32[1,512]{1,0:T(1,128)} %g_ref.1), custom_call_target="tpu_custom_call" | custom-call | flops 8589934592 | bytes 9437184 | tf_op jit(solution)/shard_map/pallas_call | solution.py:251
  70.9 1.7 %copy.8 = f32[1,1,128,512]{3,2,1,0:T(8,128)} copy(f32[1,1,128,512]{3,2,1,0:T(8,128)} %bitcast.5) | data formatting | bytes 524288

commit v2 on v1

v2 whole, which is shorter than its diff:
```python
import functools

import jax
import jax.numpy as jnp
from jax import lax
from jax.experimental import pallas as pl
from jax.experimental.pallas import tpu as pltpu
from jax.sharding import PartitionSpec as P

MESH = pl.DeviceIdType.MESH
TILE, F, NK, NM, NZ = 128, 512, 32, 8, 8
HALF = 256


def kernel(x_ref, a_hbm, mask_ref, p_ref, g_ref, o_ref,
           am, nat, ht, keep, snd, sib, cs0, cr0, cs1, cr1, xs, xr, hs, hr, bs, br, ls, lr,
           a_sem, row_s, row_r, xl_s, xl_r, agz_s, agz_r, hp_s, hp_r, xg_s, xg_r, sh_s, sh_r,
           dd_s, dd_r, xx_s, xx_r, rsz_s, rsz_r, hx_s, hx_r, br_s, br_r, lo_s, lo_r):
    r = lax.axis_index("row")
    c = lax.axis_index("col")
    xl, y = r // 4, r % 4
    z = c // 4
    h = (c // 2) % 2
    q = c % 2
    sibling = (r, c + 1 - 2 * q)
    hpartner = (r, c + 2 - 4 * h)
    lpartner = ((r + 4) % 8, c)
    zdev = ((r, (c + 4) % NK), (r, (c + 28) % NK))

    def row_at(j, same):
        return 4 * (xl if same else 1 - xl) + (y + j + 4) % 4

    def plane(d):
        return (z + d + 16) % NZ

    def block(d, hh, qq):
        return 4 * plane(d) + 2 * (h if hh == 1 else 1 - h) + qq

    sends = []

    def remote(src, dst, ssem, rsem, dev):
        return pltpu.make_async_remote_copy(
            src_ref=src, dst_ref=dst, send_sem=ssem, recv_sem=rsem,
            device_id=dev, device_id_type=MESH)

    def start(copy):
        copy.start()
        sends.append(copy)

    for m in range(NM):
        pltpu.make_async_copy(a_hbm.at[:, m], am.at[m], a_sem.at[m]).start()

    barrier = pltpu.get_barrier_semaphore()
    peers = [((row_at(j, 1)), c) for j in range(1, 4)] + [lpartner, sibling, hpartner, *zdev]
    for dev in peers:
        pl.semaphore_signal(barrier, inc=1, device_id=dev, device_id_type=MESH)

    x = x_ref[...]
    nat[r] = x.astype(jnp.bfloat16)
    ht[c] = x.T.astype(jnp.bfloat16)
    pl.semaphore_wait(barrier, len(peers))

    def ag_copy(dirn, s, hh, sending):
        d = (1 - s if sending else -s) if dirn == 0 else (s - 1 if sending else s)
        ref = ht.at[block(d, hh, q)]
        size = F if hh == 1 else HALF
        if s == 4:
            ref = ref.at[pl.ds(size // 2 * dirn, size // 2)]
        elif hh == 0:
            ref = ref.at[pl.ds(0, HALF)]
        return remote(ref, ref, agz_s.at[dirn, s - 1, hh], agz_r.at[dirn, s - 1, hh], zdev[dirn])

    def ag_send(dirn, s, hh):
        start(ag_copy(dirn, s, hh, True))

    def cross_gather(d, hh):
        ref = ht.at[block(d, hh, q)].at[pl.ds(HALF, F - HALF)]
        return remote(ref, ref, xg_s.at[d], xg_r.at[d], hpartner)

    def share(d, hh):
        ref = ht.at[block(d, hh, q)]
        start(remote(ref, ref, sh_s.at[d, hh], sh_r.at[d, hh], sibling))

    def share_wait(d, hh):
        ref = ht.at[block(d, hh, 1 - q)]
        remote(ref, ref, sh_s.at[d, hh], sh_r.at[d, hh], sibling).wait_recv()

    def ag_step(s, hh):
        for dirn in range(2):
            ag_copy(dirn, s, hh, False).wait_recv()
            if s < 4:
                ag_send(dirn, s + 1, hh)
        for d in ((8 - s, s) if s < 4 else (4,)):
            if hh == 1:
                start(cross_gather(d, 1))
            else:
                cross_gather(d, 0).wait_recv()
            share(d, hh)

    def row_copy(j, same, sending):
        ref = nat.at[row_at(0, same) if sending else row_at(-j, same)]
        return remote(ref, ref, row_s.at[j, same], row_r.at[j, same], (row_at(j, 1), c))

    def x_lo_copy(sending):
        ref = nat.at[r if sending else (r + 4) % 8]
        return remote(ref, ref, xl_s, xl_r, lpartner)

    def mask_tiles(m):
        pltpu.make_async_copy(a_hbm.at[:, m], am.at[m], a_sem.at[m]).wait()

        def body(k, carry):
            level = jnp.full((TILE, TILE), mask_ref[m, k].astype(jnp.float32))
            am[m, k] = am[m, k] * level.astype(jnp.bfloat16)
            return carry
        lax.fori_loop(0, NK, body, 0)

    ag_send(0, 1, 1)
    ag_send(1, 1, 1)
    own = ht.at[c]
    start(remote(own, own, hp_s, hp_r, hpartner))
    start(x_lo_copy(True))
    for j in (2, 1, 3):
        start(row_copy(j, 1, True))
    share(0, 1)
    for m in range(3):
        mask_tiles(m)
    other = ht.at[block(0, 0, q)]
    remote(other, other, hp_s, hp_r, hpartner).wait_recv()
    ag_send(0, 1, 0)
    ag_send(1, 1, 0)
    share(0, 0)
    x_lo_copy(False).wait_recv()
    for j in (2, 1, 3):
        start(row_copy(j, 0, True))
    for m in range(3, 6):
        mask_tiles(m)
    ag_step(1, 1)
    for m in range(6, NM):
        mask_tiles(m)
    ag_step(1, 0)
    ag_step(2, 1)
    ag_step(2, 0)
    for j in (2, 1, 3):
        for same in (1, 0):
            row_copy(j, same, False).wait_recv()

    def rows_of(k):
        return jnp.concatenate([am[m, k] for m in range(NM)], axis=1)

    def product(ds, qq):
        lhs = jnp.concatenate([rows_of(block(d, hh, qq)) for d in ds for hh in range(2)], axis=0)
        out = jnp.dot(lhs, nat[...].reshape(NM * TILE, F), preferred_element_type=jnp.float32)
        return out.reshape(len(ds), 2, TILE, F)

    def dd(d):
        return remote(snd.at[d], sib.at[d], dd_s.at[d], dd_r.at[d], sibling)

    def forward(ds):
        out = product(ds, 1 - q)
        for i, d in enumerate(ds):
            snd[d] = out[i]
            start(dd(d))
        out = product(ds, q)
        for i, d in enumerate(ds):
            keep[d] = out[i]

    def xx(d):
        return remote(xs.at[d], xr.at[d], xx_s.at[d], xx_r.at[d], hpartner)

    def cross_sums(d):
        dd(d).wait_recv()
        xs[d] = (keep[d, 0, :, HALF:] + sib[d, 0, :, HALF:]).astype(jnp.bfloat16)
        start(xx(d))

    def rsz(dirn, s, hh):
        src, dst = (cs1, cr1) if hh == 1 else (cs0, cr0)
        src, dst = src.at[dirn, s - 1], dst.at[dirn, s - 1]
        if s == 1:
            part = pl.ds(64 * dirn, 64)
            src, dst = src.at[part], dst.at[part]
        return remote(src, dst, rsz_s.at[dirn, s - 1, hh], rsz_r.at[dirn, s - 1, hh], zdev[dirn])

    def rs_step(s, hh):
        out, got = (cs1, cr1) if hh == 1 else (cs0, cr0)
        for dirn in range(2):
            d = 5 - s if dirn == 0 else 3 + s
            if hh == 1 and (s > 1 or dirn == 0):
                xx(d).wait_recv()
            if s > 1:
                rsz(dirn, s - 1, hh).wait_recv()

            def put(rows, plus):
                def sums(cols, extra):
                    value = keep[d, hh, rows, cols] + sib[d, hh, rows, cols]
                    if extra is not None:
                        value = value + extra.astype(jnp.float32)
                    if plus:
                        value = value + got[dirn, s - 2, rows, cols].astype(jnp.float32)
                    out[dirn, s - 1, rows, cols] = value.astype(jnp.bfloat16)
                sums(slice(0, HALF), None)
                if hh == 1:
                    sums(slice(HALF, F), xr[d, rows])
            lo = 64 * dirn
            if s == 1:
                put(slice(lo, lo + 64), False)
            elif s == 2:
                put(slice(lo, lo + 64), True)
                put(slice(64 - lo, 128 - lo), False)
            else:
                put(slice(0, TILE), True)
            start(rsz(dirn, s, hh))

    def brow(j, same):
        return remote(bs.at[j, same], br.at[j, same], br_s.at[j, same], br_r.at[j, same],
                      (row_at(j, 1), c))

    def backward(j):
        total = None
        for k0 in range(0, NK, 8):
            lhs = jnp.concatenate([ht[k] for k in range(k0, k0 + 8)], axis=1)
            rhs = jnp.concatenate([am[row_at(j, same), k0:k0 + 8].reshape(8 * TILE, TILE)
                                   for same in range(2)], axis=1)
            term = jnp.dot(lhs, rhs, preferred_element_type=jnp.float32)
            total = term if total is None else total + term
        for same in range(2):
            bs[j, same] = total[:, TILE * same:TILE * (same + 1)].astype(jnp.bfloat16)
            if j:
                start(brow(j, same))

    def back_sum(same):
        value = bs[0, same].astype(jnp.float32)
        for j in range(1, 4):
            brow(j, same).wait_recv()
            value = value + br[j, same].astype(jnp.float32)
        return value

    forward((4, 0))
    ag_step(3, 1)
    forward((3, 5))
    cross_sums(4)
    rs_step(1, 0)
    ag_step(3, 0)
    forward((2, 6))
    cross_sums(3)
    cross_sums(5)
    rs_step(1, 1)
    rs_step(2, 0)
    ag_step(4, 1)
    forward((1, 7))
    rs_step(2, 1)
    ag_step(4, 0)
    for d in (2, 6, 1, 7, 0):
        cross_sums(d)
    for d in range(8):
        for hh in (1, 0):
            share_wait(d, hh)
    backward(2)
    rs_step(3, 0)
    backward(1)
    rs_step(3, 1)
    backward(3)
    rs_step(4, 0)
    backward(0)
    ls[...] = back_sum(0).astype(jnp.bfloat16)
    across = remote(ls, lr, lo_s, lo_r, lpartner)
    start(across)
    rs_step(4, 1)

    for dirn in range(2):
        rsz(dirn, 4, 0).wait_recv()
    near = slice(0, HALF)
    hs[...] = (keep[0, 0, :, near] + sib[0, 0, :, near] + cr0[0, 3].astype(jnp.float32)
               + cr0[1, 3].astype(jnp.float32)).astype(jnp.bfloat16)
    cross = remote(hs, hr, hx_s, hx_r, hpartner)
    start(cross)
    back = back_sum(1)
    across.wait_recv()
    back = (back + lr[...].astype(jnp.float32)).T
    xx(0).wait_recv()
    for dirn in range(2):
        rsz(dirn, 4, 1).wait_recv()
    cross.wait_recv()
    far = jnp.concatenate([hr[...], xr[0]], axis=1).astype(jnp.float32)
    summed = (keep[0, 1] + sib[0, 1] + far + cr1[0, 3].astype(jnp.float32)
              + cr1[1, 3].astype(jnp.float32) + back)
    mixed = jnp.dot(summed, p_ref[...], precision=lax.Precision.HIGHEST,
                    preferred_element_type=jnp.float32)
    lifted = x_ref[...] + jnp.maximum(mixed, 0.0)
    scale = lax.rsqrt(jnp.mean(lifted * lifted, axis=-1, keepdims=True) + 1e-06)
    o_ref[...] = lifted * scale * g_ref[...]
    for copy in sends:
        copy.wait_send()


def shards(features, adjacency, tile_mask, projection, row_gain):
    vm = pl.BlockSpec(memory_space=pltpu.VMEM)
    bf, f32 = jnp.bfloat16, jnp.float32
    dma = pltpu.SemaphoreType.DMA
    out = pl.pallas_call(
        kernel,
        out_shape=jax.ShapeDtypeStruct((TILE, F), f32),
        in_specs=[vm, pl.BlockSpec(memory_space=pl.ANY),
                  pl.BlockSpec(memory_space=pltpu.SMEM), vm, vm],
        out_specs=vm,
        scratch_shapes=[
            pltpu.VMEM((NM, NK, TILE, TILE), bf),
            pltpu.VMEM((8, TILE, F), bf),
            pltpu.VMEM((NK, F, TILE), bf),
            pltpu.VMEM((8, 2, TILE, F), f32),
            pltpu.VMEM((8, 2, TILE, F), f32),
            pltpu.VMEM((8, 2, TILE, F), f32),
            pltpu.VMEM((2, 4, TILE, HALF), bf),
            pltpu.VMEM((2, 4, TILE, HALF), bf),
            pltpu.VMEM((2, 4, TILE, F), bf),
            pltpu.VMEM((2, 4, TILE, F), bf),
            pltpu.VMEM((8, TILE, F - HALF), bf),
            pltpu.VMEM((8, TILE, F - HALF), bf),
            pltpu.VMEM((TILE, HALF), bf),
            pltpu.VMEM((TILE, HALF), bf),
            pltpu.VMEM((4, 2, F, TILE), bf),
            pltpu.VMEM((4, 2, F, TILE), bf),
            pltpu.VMEM((F, TILE), bf),
            pltpu.VMEM((F, TILE), bf),
            dma((NM,)), dma((4, 2)), dma((4, 2)), dma, dma, dma((2, 4, 2)), dma((2, 4, 2)),
            dma, dma, dma((8,)), dma((8,)), dma((8, 2)), dma((8, 2)),
            dma((8,)), dma((8,)), dma((8,)), dma((8,)), dma((2, 4, 2)), dma((2, 4, 2)),
            dma, dma, dma((4, 2)), dma((4, 2)), dma, dma,
        ],
        compiler_params=pltpu.CompilerParams(
            collective_id=0, has_side_effects=True, vmem_limit_bytes=56 * 2**20),
        cost_estimate=pl.CostEstimate(
            flops=4 * 32 * 1024 * 128 * 512, bytes_accessed=9 * 2**20, transcendentals=128),
    )(features[0, 0], adjacency[:, 0, 0], tile_mask[:, 0, 0].T, projection[0], row_gain)
    return out[None, None]


def solution(mesh):
    return jax.shard_map(
        shards,
        mesh=mesh,
        in_specs=(
            P("col", "row", None, None),
            P(None, "row", "col", None, None, None),
            P(None, "row", "col", None),
            P(),
            P(),
        ),
        out_specs=P("col", "row", None, None),
        check_vma=False,
    )
```

time: 72.8 us -> 69.6 us (0.956)
  Pallas kernels: 69.6 us -> 67.8 us
  local copies, waits for them, and re-layouts: 3.04 us -> 1.67 us
    pallas_call x1, Pallas kernels: 69.6 us -> 67.8 us  [shards(): pl.pallas_call(kernel, out_shape=jax.ShapeDtypeStruct((TILE, F), f32), in...]
    unnamed x2 -> x1, local copies, waits for them, and re-layouts: 3.04 us -> 1.67 us
where the time goes in v2:
time: 69.6 us; the launch traced here: 69.5 us
  Pallas kernels  67.8 us (97%)
  local copies, waits for them, and re-layouts  1.67 us (2%)
    pallas_call x1, Pallas kernels, shards(): pl.pallas_call(kernel, out_shape=jax.ShapeDtypeStruct((TILE, F), f32), in...  67.8 us
    unnamed x1, local copies, waits for them, and re-layouts  1.67 us

profile of v2, /device:TPU:1, one launch (start us, length us, event | category | flops | bytes accessed | tf_op | source)
XLA Modules:
  0.0 69.5 jit_solution(17108495062880106232)
XLA Ops:
  0.0 67.8 %shard_map.55 = f32[128,512]{1,0:T(8,128)} custom-call(f32[128,512]{1,0:T(8,128)} %bitcast.10, bf16[32,8,128,128]{3,2,1,0:T(8,128)(2,1)} %bitcast.8, s32[8,32]{1,0:T(8,128)} %bitcast.11, f32[512,512]{1,0:T(8,128)} %bitcast.9, f32[1,512]{1,0:T(1,128)} %g_ref.1), custom_call_target="tpu_custom_call" | custom-call | flops 8589934592 | bytes 9437184 | tf_op jit(solution)/shard_map/pallas_call | solution.py:299
  67.8 1.7 %copy.7 = f32[1,1,128,512]{3,2,1,0:T(8,128)} copy(f32[1,1,128,512]{3,2,1,0:T(8,128)} %bitcast.7) | data formatting | bytes 524288

commit v3 on v2

--- a/solution.py
+++ b/solution.py
@@ -13,7 +13,7 @@
 
 
 def kernel(x_ref, a_hbm, mask_ref, p_ref, g_ref, o_ref,
-           am, nat, ht, keep, snd, sib, cs0, cr0, cs1, cr1, xs, xr, hs, hr, bs, br, ls, lr,
+           am, nat, ht, keep, snd, sib, cs0, cr0, cs1, cr1, xs, xr, hs, hr, acc, bs, br, ls, lr,
            a_sem, row_s, row_r, xl_s, xl_r, agz_s, agz_r, hp_s, hp_r, xg_s, xg_r, sh_s, sh_r,
            dd_s, dd_r, xx_s, xx_r, rsz_s, rsz_r, hx_s, hx_r, br_s, br_r, lo_s, lo_r):
     r = lax.axis_index("row")
@@ -60,18 +60,20 @@
     ht[c] = x.T.astype(jnp.bfloat16)
     pl.semaphore_wait(barrier, len(peers))
 
-    def ag_copy(dirn, s, hh, sending):
+    def ag_ways(s, p):
+        return (0, 1) if s < 4 or p == 2 else ((1,) if p == 0 else (0,))
+
+    def ag_copy(dirn, s, p, sending):
         d = (1 - s if sending else -s) if dirn == 0 else (s - 1 if sending else s)
-        ref = ht.at[block(d, hh, q)]
-        size = F if hh == 1 else HALF
-        if s == 4:
-            ref = ref.at[pl.ds(size // 2 * dirn, size // 2)]
-        elif hh == 0:
-            ref = ref.at[pl.ds(0, HALF)]
-        return remote(ref, ref, agz_s.at[dirn, s - 1, hh], agz_r.at[dirn, s - 1, hh], zdev[dirn])
-
-    def ag_send(dirn, s, hh):
-        start(ag_copy(dirn, s, hh, True))
+        lo, size = (HALF, HALF) if p == 0 else (0, HALF)
+        if p == 2 and s == 4:
+            lo, size = HALF // 2 * dirn, HALF // 2
+        ref = ht.at[block(d, 0 if p == 2 else 1, q)].at[pl.ds(lo, size)]
+        return remote(ref, ref, agz_s.at[dirn, s - 1, p], agz_r.at[dirn, s - 1, p], zdev[dirn])
+
+    def ag_send(s, p):
+        for dirn in ag_ways(s, p):
+            start(ag_copy(dirn, s, p, True))
 
     def cross_gather(d, hh):
         ref = ht.at[block(d, hh, q)].at[pl.ds(HALF, F - HALF)]
@@ -81,21 +83,25 @@
         ref = ht.at[block(d, hh, q)]
         start(remote(ref, ref, sh_s.at[d, hh], sh_r.at[d, hh], sibling))
 
-    def share_wait(d, hh):
-        ref = ht.at[block(d, hh, 1 - q)]
-        remote(ref, ref, sh_s.at[d, hh], sh_r.at[d, hh], sibling).wait_recv()
-
-    def ag_step(s, hh):
-        for dirn in range(2):
-            ag_copy(dirn, s, hh, False).wait_recv()
-            if s < 4:
-                ag_send(dirn, s + 1, hh)
+    def share_wait(*ds):
+        for d in ds:
+            for hh in (1, 0):
+                ref = ht.at[block(d, hh, 1 - q)]
+                remote(ref, ref, sh_s.at[d, hh], sh_r.at[d, hh], sibling).wait_recv()
+
+    def ag_step(s, p):
+        for dirn in ag_ways(s, p):
+            ag_copy(dirn, s, p, False).wait_recv()
+            if s < 4 and dirn in ag_ways(s + 1, p):
+                start(ag_copy(dirn, s + 1, p, True))
         for d in ((8 - s, s) if s < 4 else (4,)):
-            if hh == 1:
+            if p == 0:
                 start(cross_gather(d, 1))
+            elif p == 1:
+                share(d, 1)
             else:
                 cross_gather(d, 0).wait_recv()
-            share(d, hh)
+                share(d, 0)
 
     def row_copy(j, same, sending):
         ref = nat.at[row_at(0, same) if sending else row_at(-j, same)]
@@ -114,32 +120,55 @@
             return carry
         lax.fori_loop(0, NK, body, 0)
 
-    ag_send(0, 1, 1)
-    ag_send(1, 1, 1)
+    def back_pass(js, ds, first):
+        ks = [block(d, hh, qq) for d in ds for hh in range(2) for qq in (q, 1 - q)]
+        for j in js:
+            lhs = jnp.concatenate([ht[k] for k in ks], axis=1)
+            rhs = jnp.concatenate(
+                [jnp.concatenate([am[row_at(j, same), k] for k in ks], axis=0)
+                 for same in range(2)], axis=1)
+            term = jnp.dot(lhs, rhs, preferred_element_type=jnp.float32)
+            acc[j] = term if first else acc[j] + term
+
+    ag_send(1, 0)
+    ag_send(1, 1)
     own = ht.at[c]
     start(remote(own, own, hp_s, hp_r, hpartner))
     start(x_lo_copy(True))
     for j in (2, 1, 3):
         start(row_copy(j, 1, True))
     share(0, 1)
-    for m in range(3):
+    for m in range(2):
         mask_tiles(m)
+    ag_step(1, 0)
+    mask_tiles(2)
     other = ht.at[block(0, 0, q)]
     remote(other, other, hp_s, hp_r, hpartner).wait_recv()
-    ag_send(0, 1, 0)
-    ag_send(1, 1, 0)
+    ag_send(1, 2)
     share(0, 0)
     x_lo_copy(False).wait_recv()
     for j in (2, 1, 3):
         start(row_copy(j, 0, True))
-    for m in range(3, 6):
-        mask_tiles(m)
     ag_step(1, 1)
-    for m in range(6, NM):
-        mask_tiles(m)
-    ag_step(1, 0)
+    mask_tiles(3)
+    mask_tiles(4)
+    ag_step(2, 0)
+    mask_tiles(5)
+    mask_tiles(6)
     ag_step(2, 1)
-    ag_step(2, 0)
+    mask_tiles(7)
+    ag_step(1, 2)
+    ag_step(3, 0)
+    share_wait(0)
+    back_pass((2, 1), (0,), True)
+    ag_step(3, 1)
+    back_pass((3, 0), (0,), True)
+    ag_step(2, 2)
+    share_wait(1, 7)
+    back_pass((2, 1), (1, 7), False)
+    ag_step(4, 0)
+    back_pass((3, 0), (1, 7), False)
+    ag_step(4, 1)
     for j in (2, 1, 3):
         for same in (1, 0):
             row_copy(j, same, False).wait_recv()
@@ -172,24 +201,32 @@
         xs[d] = (keep[d, 0, :, HALF:] + sib[d, 0, :, HALF:]).astype(jnp.bfloat16)
         start(xx(d))
 
-    def rsz(dirn, s, hh):
-        src, dst = (cs1, cr1) if hh == 1 else (cs0, cr0)
-        src, dst = src.at[dirn, s - 1], dst.at[dirn, s - 1]
-        if s == 1:
-            part = pl.ds(64 * dirn, 64)
-            src, dst = src.at[part], dst.at[part]
-        return remote(src, dst, rsz_s.at[dirn, s - 1, hh], rsz_r.at[dirn, s - 1, hh], zdev[dirn])
-
-    def rs_step(s, hh):
-        out, got = (cs1, cr1) if hh == 1 else (cs0, cr0)
-        for dirn in range(2):
+    def rs_ways(s, p):
+        return (0, 1) if s > 1 or p == 0 else (p - 1,)
+
+    def rs_rows(dirn, s, p):
+        if p == 0:
+            return (64 * dirn, 64) if s == 1 else (0, TILE)
+        return (64 * (p - 1), 64)
+
+    def rsz(dirn, s, p):
+        src, dst = (cs0, cr0) if p == 0 else (cs1, cr1)
+        part = pl.ds(*rs_rows(dirn, s, p))
+        return remote(src.at[dirn, s - 1].at[part], dst.at[dirn, s - 1].at[part],
+                      rsz_s.at[dirn, s - 1, p], rsz_r.at[dirn, s - 1, p], zdev[dirn])
+
+    def rs_step(s, p):
+        out, got = (cs0, cr0) if p == 0 else (cs1, cr1)
+        hh = 0 if p == 0 else 1
+        for dirn in rs_ways(s, p):
             d = 5 - s if dirn == 0 else 3 + s
-            if hh == 1 and (s > 1 or dirn == 0):
-                xx(d).wait_recv()
-            if s > 1:
-                rsz(dirn, s - 1, hh).wait_recv()
-
-            def put(rows, plus):
+            received = s > 1 and dirn in rs_ways(s - 1, p)
+            if received:
+                rsz(dirn, s - 1, p).wait_recv()
+
+            def put(lo, size, plus):
+                rows = slice(lo, lo + size)
+
                 def sums(cols, extra):
                     value = keep[d, hh, rows, cols] + sib[d, hh, rows, cols]
                     if extra is not None:
@@ -200,30 +237,21 @@
                 sums(slice(0, HALF), None)
                 if hh == 1:
                     sums(slice(HALF, F), xr[d, rows])
-            lo = 64 * dirn
-            if s == 1:
-                put(slice(lo, lo + 64), False)
-            elif s == 2:
-                put(slice(lo, lo + 64), True)
-                put(slice(64 - lo, 128 - lo), False)
+            if p == 0 and s == 2:
+                put(64 * dirn, 64, True)
+                put(64 - 64 * dirn, 64, False)
             else:
-                put(slice(0, TILE), True)
-            start(rsz(dirn, s, hh))
+                put(*rs_rows(dirn, s, p), received)
+            start(rsz(dirn, s, p))
 
     def brow(j, same):
         return remote(bs.at[j, same], br.at[j, same], br_s.at[j, same], br_r.at[j, same],
                       (row_at(j, 1), c))
 
     def backward(j):
-        total = None
-        for k0 in range(0, NK, 8):
-            lhs = jnp.concatenate([ht[k] for k in range(k0, k0 + 8)], axis=1)
-            rhs = jnp.concatenate([am[row_at(j, same), k0:k0 + 8].reshape(8 * TILE, TILE)
-                                   for same in range(2)], axis=1)
-            term = jnp.dot(lhs, rhs, preferred_element_type=jnp.float32)
-            total = term if total is None else total + term
+        back_pass((j,), (2, 6, 3, 5, 4), False)
         for same in range(2):
-            bs[j, same] = total[:, TILE * same:TILE * (same + 1)].astype(jnp.bfloat16)
+            bs[j, same] = acc[j, :, TILE * same:TILE * (same + 1)].astype(jnp.bfloat16)
             if j:
                 start(brow(j, same))
 
@@ -235,36 +263,46 @@
         return value
 
     forward((4, 0))
-    ag_step(3, 1)
+    ag_step(3, 2)
     forward((3, 5))
     cross_sums(4)
     rs_step(1, 0)
-    ag_step(3, 0)
+    ag_step(4, 2)
     forward((2, 6))
     cross_sums(3)
     cross_sums(5)
+    xx(4).wait_recv()
     rs_step(1, 1)
+    rs_step(1, 2)
     rs_step(2, 0)
-    ag_step(4, 1)
     forward((1, 7))
+    share_wait(2, 6, 3, 5, 4)
+    backward(2)
+    cross_sums(2)
+    cross_sums(6)
+    xx(3).wait_recv()
+    xx(5).wait_recv()
     rs_step(2, 1)
-    ag_step(4, 0)
-    for d in (2, 6, 1, 7, 0):
-        cross_sums(d)
-    for d in range(8):
-        for hh in (1, 0):
-            share_wait(d, hh)
-    backward(2)
+    rs_step(2, 2)
+    backward(1)
+    cross_sums(1)
+    cross_sums(7)
+    cross_sums(0)
     rs_step(3, 0)
-    backward(1)
+    backward(3)
+    xx(2).wait_recv()
+    xx(6).wait_recv()
     rs_step(3, 1)
-    backward(3)
+    rs_step(3, 2)
+    backward(0)
     rs_step(4, 0)
-    backward(0)
+    xx(1).wait_recv()
+    xx(7).wait_recv()
+    rs_step(4, 1)
+    rs_step(4, 2)
     ls[...] = back_sum(0).astype(jnp.bfloat16)
     across = remote(ls, lr, lo_s, lo_r, lpartner)
     start(across)
-    rs_step(4, 1)
 
     for dirn in range(2):
         rsz(dirn, 4, 0).wait_recv()
@@ -279,6 +317,7 @@
     xx(0).wait_recv()
     for dirn in range(2):
         rsz(dirn, 4, 1).wait_recv()
+        rsz(dirn, 4, 2).wait_recv()
     cross.wait_recv()
     far = jnp.concatenate([hr[...], xr[0]], axis=1).astype(jnp.float32)
     summed = (keep[0, 1] + sib[0, 1] + far + cr1[0, 3].astype(jnp.float32)
@@ -317,13 +356,14 @@
             pltpu.VMEM((8, TILE, F - HALF), bf),
             pltpu.VMEM((TILE, HALF), bf),
             pltpu.VMEM((TILE, HALF), bf),
+            pltpu.VMEM((4, F, 2 * TILE), f32),
             pltpu.VMEM((4, 2, F, TILE), bf),
             pltpu.VMEM((4, 2, F, TILE), bf),
             pltpu.VMEM((F, TILE), bf),
             pltpu.VMEM((F, TILE), bf),
-            dma((NM,)), dma((4, 2)), dma((4, 2)), dma, dma, dma((2, 4, 2)), dma((2, 4, 2)),
+            dma((NM,)), dma((4, 2)), dma((4, 2)), dma, dma, dma((2, 4, 3)), dma((2, 4, 3)),
             dma, dma, dma((8,)), dma((8,)), dma((8, 2)), dma((8, 2)),
-            dma((8,)), dma((8,)), dma((8,)), dma((8,)), dma((2, 4, 2)), dma((2, 4, 2)),
+            dma((8,)), dma((8,)), dma((8,)), dma((8,)), dma((2, 4, 3)), dma((2, 4, 3)),
             dma, dma, dma((4, 2)), dma((4, 2)), dma, dma,
         ],
         compiler_params=pltpu.CompilerParams(

time: 69.6 us -> 61.2 us (0.88)
  Pallas kernels: 67.8 us -> 58.8 us
    pallas_call x1, Pallas kernels: 67.8 us -> 58.8 us  [shards(): pl.pallas_call(kernel, out_shape=jax.ShapeDtypeStruct((TILE, F), f32), in...]
where the time goes in v3:
time: 61.2 us; the launch traced here: 60.5 us
  Pallas kernels  58.8 us (96%)
  local copies, waits for them, and re-layouts  1.67 us (3%)
    pallas_call x1, Pallas kernels, shards(): pl.pallas_call(kernel, out_shape=jax.ShapeDtypeStruct((TILE, F), f32), in...  58.8 us
    unnamed x1, local copies, waits for them, and re-layouts  1.67 us

profile of v3, /device:TPU:1, one launch (start us, length us, event | category | flops | bytes accessed | tf_op | source)
XLA Modules:
  0.0 60.5 jit_solution(14830673209768960901)
XLA Ops:
  0.0 58.8 %shard_map.55 = f32[128,512]{1,0:T(8,128)} custom-call(f32[128,512]{1,0:T(8,128)} %bitcast.10, bf16[32,8,128,128]{3,2,1,0:T(8,128)(2,1)} %bitcast.8, s32[8,32]{1,0:T(8,128)} %bitcast.11, f32[512,512]{1,0:T(8,128)} %bitcast.9, f32[1,512]{1,0:T(1,128)} %g_ref.1), custom_call_target="tpu_custom_call" | custom-call | flops 8589934592 | bytes 9437184 | tf_op jit(solution)/shard_map/pallas_call | solution.py:338
  58.8 1.7 %copy.7 = f32[1,1,128,512]{3,2,1,0:T(8,128)} copy(f32[1,1,128,512]{3,2,1,0:T(8,128)} %bitcast.7) | data formatting | bytes 524288

commit v4 on v3

v4 whole, which is shorter than its diff:
```python
import functools

import jax
import jax.numpy as jnp
from jax import lax
from jax.experimental import pallas as pl
from jax.experimental.pallas import tpu as pltpu
from jax.sharding import PartitionSpec as P

MESH = pl.DeviceIdType.MESH
TILE, F, NK, NM, NZ = 128, 512, 32, 8, 8
HALF = 256


def kernel(x_ref, a_hbm, mask_ref, p_ref, g_ref, o_ref,
           am, nat, ht, keep, snd, sib, cs0, cr0, cs1, cr1, xs, xr, hs, hr, acc, bs, br, ts, tr,
           ns, nr, a_sem, row_s, row_r, xl_s, xl_r, agz_s, agz_r, hp_s, hp_r, xg_s, xg_r, sh_s, sh_r,
           dd_s, dd_r, xx_s, xx_r, rsz_s, rsz_r, hx_s, hx_r, br_s, br_r, tt_s, tt_r,
           cg_s, cg_r, cn_s, cn_r):
    r = lax.axis_index("row")
    c = lax.axis_index("col")
    xl, y = r // 4, r % 4
    z = c // 4
    h = (c // 2) % 2
    q = c % 2
    sibling = (r, c + 1 - 2 * q)
    hpartner = (r, c + 2 - 4 * h)
    lpartner = ((r + 4) % 8, c)
    zdev = ((r, (c + 4) % NK), (r, (c + 28) % NK))

    def row_at(j, same):
        return 4 * (xl if same else 1 - xl) + (y + j + 4) % 4

    def plane(d):
        return (z + d + 16) % NZ

    def block(d, hh, qq):
        return 4 * plane(d) + 2 * (h if hh == 1 else 1 - h) + qq

    opposite = (r, block(4, 1, q))
    corner = (r, block(4, 0, 1 - q))
    at_corner = jnp.logical_and(h == q, jnp.logical_or(
        jnp.logical_and(h == 1, z < 4), jnp.logical_and(h == 0, z >= 4)))
    zdiag = tuple((r, block(d, 0, q)) for d in (1, -1))

    sends = []

    def remote(src, dst, ssem, rsem, dev):
        return pltpu.make_async_remote_copy(
            src_ref=src, dst_ref=dst, send_sem=ssem, recv_sem=rsem,
            device_id=dev, device_id_type=MESH)

    def start(copy):
        copy.start()
        sends.append(copy)

    for m in range(NM):
        pltpu.make_async_copy(a_hbm.at[:, m], am.at[m], a_sem.at[m]).start()

    barrier = pltpu.get_barrier_semaphore()
    peers = ([((r + j) % 8, c) for j in range(1, 8)]
             + [sibling, hpartner, opposite, corner, *zdev, *zdiag])
    for dev in peers:
        pl.semaphore_signal(barrier, inc=1, device_id=dev, device_id_type=MESH)

    x = x_ref[...]
    nat[r] = x.astype(jnp.bfloat16)
    ht[c] = x.T.astype(jnp.bfloat16)
    pl.semaphore_wait(barrier, len(peers))

    @pl.when(jnp.logical_not(at_corner))
    def _():
        ht[corner[1]] = jnp.zeros((F, TILE), jnp.bfloat16)

    def ag_ways(s, p):
        return (0, 1) if s < 4 else ((1,), (0,), ())[p]

    def ag_copy(dirn, s, p, sending):
        d = (1 - s if sending else -s) if dirn == 0 else (s - 1 if sending else s)
        lo, size = (HALF, HALF) if p == 0 else (0, HALF)
        hh, dev = (0 if p == 2 else 1), zdev[dirn]
        if p == 2 and s == 1 and sending:
            hh, dev = 1, zdiag[dirn]
        ref = ht.at[block(d, hh, q)].at[pl.ds(lo, size)]
        return remote(ref, ref, agz_s.at[dirn, s - 1, p], agz_r.at[dirn, s - 1, p], dev)

    def ag_send(s, p):
        for dirn in ag_ways(s, p):
            start(ag_copy(dirn, s, p, True))

    def cross_gather(d, hh):
        ref = ht.at[block(d, hh, q)].at[pl.ds(HALF, F - HALF)]
        return remote(ref, ref, xg_s.at[d], xg_r.at[d], hpartner)

    def share(d, hh):
        ref = ht.at[block(d, hh, q)]
        start(remote(ref, ref, sh_s.at[d, hh], sh_r.at[d, hh], sibling))

    def share_wait(*ds):
        for d in ds:
            for hh in (1, 0):
                ref = ht.at[block(d, hh, 1 - q)]
                remote(ref, ref, sh_s.at[d, hh], sh_r.at[d, hh], sibling).wait_recv()

    def ag_step(s, p):
        for dirn in ag_ways(s, p):
            ag_copy(dirn, s, p, False).wait_recv()
            if s < 4 and dirn in ag_ways(s + 1, p):
                start(ag_copy(dirn, s + 1, p, True))
        for d in ((8 - s, s) if s < 4 else ()):
            if p == 0:
                start(cross_gather(d, 1))
            elif p == 1:
                share(d, 1)
            else:
                cross_gather(d, 0).wait_recv()
                share(d, 0)

    def row_copy(j, same, sending):
        ref = nat.at[row_at(0, same) if sending else row_at(-j, same)]
        return remote(ref, ref, row_s.at[j, same], row_r.at[j, same], (row_at(j, 1), c))

    def x_lo_copy(sending):
        ref = nat.at[r if sending else (r + 4) % 8]
        return remote(ref, ref, xl_s, xl_r, lpartner)

    def mask_tiles(m):
        pltpu.make_async_copy(a_hbm.at[:, m], am.at[m], a_sem.at[m]).wait()

        def body(k, carry):
            level = jnp.full((TILE, TILE), mask_ref[m, k].astype(jnp.float32))
            am[m, k] = am[m, k] * level.astype(jnp.bfloat16)
            return carry
        lax.fori_loop(0, NK, body, 0)

    def back_pass(js, ds, first):
        ks = [block(d, hh, qq) for d in ds for hh in range(2) for qq in (q, 1 - q)
              if d != 4 or (hh, qq is q) in ((1, True), (0, False))]
        for j in js:
            lhs = jnp.concatenate([ht[k] for k in ks], axis=1)
            rhs = jnp.concatenate(
                [jnp.concatenate([am[row_at(j, same), k] for k in ks], axis=0)
                 for same in range(2)], axis=1)
            term = jnp.dot(lhs, rhs, preferred_element_type=jnp.float32)
            acc[j] = term if first else acc[j] + term

    own = ht.at[c]
    start(x_lo_copy(True))
    for j in (2, 1, 3):
        start(row_copy(j, 1, True))
    for p in range(3):
        ag_send(1, p)
    share(0, 1)
    corner_gather = remote(own, own, cg_s, cg_r, corner)

    @pl.when(at_corner)
    def _():
        corner_gather.start()
    for m in range(5):
        mask_tiles(m)
    ag_step(1, 0)
    mask_tiles(5)
    mask_tiles(6)
    x_lo_copy(False).wait_recv()
    for j in (2, 1, 3):
        start(row_copy(j, 0, True))
    start(remote(own, own, hp_s, hp_r, hpartner))
    ag_step(1, 1)
    mask_tiles(7)
    ts[...] = am[r, opposite[1]]
    tile_copy = remote(ts, tr, tt_s, tt_r, opposite)
    start(tile_copy)
    ag_step(2, 0)
    ag_step(1, 2)
    ag_step(2, 1)
    other = ht.at[block(0, 0, q)]
    remote(other, other, hp_s, hp_r, hpartner).wait_recv()
    share(0, 0)
    ag_step(3, 0)
    ag_step(2, 2)
    share_wait(0)
    back_pass((2, 1, 3, 0), (0,), True)
    ag_step(3, 1)
    share_wait(1, 7)
    back_pass((2, 1), (1, 7), False)
    for j in (2, 1, 3):
        for same in (1, 0):
            row_copy(j, same, False).wait_recv()

    def rows_of(k):
        return jnp.concatenate([am[m, k] for m in range(NM)], axis=1)

    def product(ds, qq):
        lhs = jnp.concatenate([rows_of(block(d, hh, qq)) for d in ds for hh in range(2)], axis=0)
        out = jnp.dot(lhs, nat[...].reshape(NM * TILE, F), preferred_element_type=jnp.float32)
        return out.reshape(len(ds), 2, TILE, F)

    def dd(d, hh):
        return remote(snd.at[d, hh], sib.at[d, hh], dd_s.at[d, hh], dd_r.at[d, hh], sibling)

    def forward(ds):
        out = product(ds, 1 - q)
        for i, d in enumerate(ds):
            snd[d] = out[i]
            start(dd(d, 0))
        for d in ds:
            start(dd(d, 1))
        out = product(ds, q)
        for i, d in enumerate(ds):
            keep[d] = out[i]

    def xx(d):
        return remote(xs.at[d], xr.at[d], xx_s.at[d], xx_r.at[d], hpartner)

    def cross_sums(d):
        dd(d, 0).wait_recv()
        xs[d] = (keep[d, 0, :, HALF:] + sib[d, 0, :, HALF:]).astype(jnp.bfloat16)
        start(xx(d))

    def rs_rows(p):
        return (0, TILE) if p == 0 else (64 * (p - 1), 64)

    def rsz(dirn, s, p):
        src, dst = (cs0, cr0) if p == 0 else (cs1, cr1)
        part = pl.ds(*rs_rows(p))
        return remote(src.at[dirn, s - 1].at[part], dst.at[dirn, s - 1].at[part],
                      rsz_s.at[dirn, s - 1, p], rsz_r.at[dirn, s - 1, p], zdev[dirn])

    def rs_step(s, p):
        out, got = (cs0, cr0) if p == 0 else (cs1, cr1)
        hh = 0 if p == 0 else 1
        lo, size = rs_rows(p)
        rows = slice(lo, lo + size)
        for dirn in range(2):
            d = 5 - s if dirn == 0 else 3 + s
            if p == 1:
                dd(d, 1).wait_recv()
                xx(d).wait_recv()
            if s > 2:
                rsz(dirn, s - 1, p).wait_recv()

            def sums(cols, extra):
                value = keep[d, hh, rows, cols] + sib[d, hh, rows, cols]
                if extra is not None:
                    value = value + extra.astype(jnp.float32)
                if s > 2:
                    value = value + got[dirn, s - 2, rows, cols].astype(jnp.float32)
                out[dirn, s - 1, rows, cols] = value.astype(jnp.bfloat16)
            sums(slice(0, HALF), None)
            if hh == 1:
                sums(slice(HALF, F), xr[d, rows])
            start(rsz(dirn, s, p))

    def brow(j, same, sending=True):
        dev = (row_at(j if sending else -j, same), c)
        return remote(bs.at[j, same], br.at[j, same], br_s.at[j, same], br_r.at[j, same], dev)

    def backward(j):
        back_pass((j,), (2, 6, 3, 5, 4), False)
        for same in range(2):
            bs[j, same] = acc[j, :, TILE * same:TILE * (same + 1)].astype(jnp.bfloat16)
            if j or not same:
                start(brow(j, same))

    corner_sums = remote(ns, nr, cn_s, cn_r, corner)

    def corner_product():
        @pl.when(at_corner)
        def _():
            ns[...] = jnp.dot(rows_of(corner[1]), nat[...].reshape(NM * TILE, F),
                              preferred_element_type=jnp.float32).astype(jnp.bfloat16)
            corner_sums.start()

    forward((3, 5))
    back_pass((3, 0), (1, 7), False)
    forward((2, 6))
    ag_step(3, 2)
    for p in range(2):
        ag_step(4, p)
    cross_sums(3)
    cross_sums(5)
    rs_step(2, 0)
    forward((1, 7))
    corner_product()
    share_wait(2, 6, 3, 5)

    @pl.when(at_corner)
    def _():
        corner_gather.wait_recv()
    backward(2)
    cross_sums(2)
    cross_sums(6)
    rs_step(2, 1)
    rs_step(2, 2)
    backward(1)
    cross_sums(1)
    cross_sums(7)
    rs_step(3, 0)
    backward(3)
    rs_step(3, 1)
    rs_step(3, 2)
    backward(0)
    forward((0,))
    rs_step(4, 0)
    cross_sums(0)
    rs_step(4, 1)
    rs_step(4, 2)

    back = acc[0, :, TILE:]
    tile_copy.wait_recv()
    back = back + lax.dot_general(ht[opposite[1]], tr[...], (((1,), (1,)), ((), ())),
                                  preferred_element_type=jnp.float32)
    for j in (2, 1, 3, 0):
        for same in range(2):
            if j or not same:
                brow(j, same, False).wait_recv()
                back = back + br[j, same].astype(jnp.float32)
    dd(0, 1).wait_recv()
    keep[0, 1] = keep[0, 1] + sib[0, 1] + back.T

    @pl.when(at_corner)
    def _():
        corner_sums.wait_recv()
        keep[0, 1] = keep[0, 1] + nr[...].astype(jnp.float32)
    for dirn in range(2):
        rsz(dirn, 4, 0).wait_recv()
    near = slice(0, HALF)
    hs[...] = (keep[0, 0, :, near] + sib[0, 0, :, near] + cr0[0, 3].astype(jnp.float32)
               + cr0[1, 3].astype(jnp.float32)).astype(jnp.bfloat16)
    cross = remote(hs, hr, hx_s, hx_r, hpartner)
    start(cross)
    xx(0).wait_recv()
    for p in (1, 2):
        for dirn in range(2):
            rsz(dirn, 4, p).wait_recv()
    summed = keep[0, 1] + cr1[0, 3].astype(jnp.float32) + cr1[1, 3].astype(jnp.float32)
    cross.wait_recv()
    summed = summed + jnp.concatenate([hr[...], xr[0]], axis=1).astype(jnp.float32)
    mixed = jnp.dot(summed, p_ref[...], precision=lax.Precision.HIGHEST,
                    preferred_element_type=jnp.float32)
    lifted = x_ref[...] + jnp.maximum(mixed, 0.0)
    scale = lax.rsqrt(jnp.mean(lifted * lifted, axis=-1, keepdims=True) + 1e-06)
    o_ref[...] = lifted * scale * g_ref[...]
    for copy in sends:
        copy.wait_send()

    @pl.when(at_corner)
    def _():
        corner_gather.wait_send()
        corner_sums.wait_send()


def shards(features, adjacency, tile_mask, projection, row_gain):
    vm = pl.BlockSpec(memory_space=pltpu.VMEM)
    bf, f32 = jnp.bfloat16, jnp.float32
    dma = pltpu.SemaphoreType.DMA
    out = pl.pallas_call(
        kernel,
        out_shape=jax.ShapeDtypeStruct((TILE, F), f32),
        in_specs=[vm, pl.BlockSpec(memory_space=pl.ANY),
                  pl.BlockSpec(memory_space=pltpu.SMEM), vm, vm],
        out_specs=vm,
        scratch_shapes=[
            pltpu.VMEM((NM, NK, TILE, TILE), bf),
            pltpu.VMEM((8, TILE, F), bf),
            pltpu.VMEM((NK, F, TILE), bf),
            pltpu.VMEM((8, 2, TILE, F), f32),
            pltpu.VMEM((8, 2, TILE, F), f32),
            pltpu.VMEM((8, 2, TILE, F), f32),
            pltpu.VMEM((2, 4, TILE, HALF), bf),
            pltpu.VMEM((2, 4, TILE, HALF), bf),
            pltpu.VMEM((2, 4, TILE, F), bf),
            pltpu.VMEM((2, 4, TILE, F), bf),
            pltpu.VMEM((8, TILE, F - HALF), bf),
            pltpu.VMEM((8, TILE, F - HALF), bf),
            pltpu.VMEM((TILE, HALF), bf),
            pltpu.VMEM((TILE, HALF), bf),
            pltpu.VMEM((4, F, 2 * TILE), f32),
            pltpu.VMEM((4, 2, F, TILE), bf),
            pltpu.VMEM((4, 2, F, TILE), bf),
            pltpu.VMEM((TILE, TILE), bf),
            pltpu.VMEM((TILE, TILE), bf),
            pltpu.VMEM((TILE, F), bf),
            pltpu.VMEM((TILE, F), bf),
            dma((NM,)), dma((4, 2)), dma((4, 2)), dma, dma, dma((2, 4, 3)), dma((2, 4, 3)),
            dma, dma, dma((8,)), dma((8,)), dma((8, 2)), dma((8, 2)),
            dma((8, 2)), dma((8, 2)), dma((8,)), dma((8,)), dma((2, 4, 3)), dma((2, 4, 3)),
            dma, dma, dma((4, 2)), dma((4, 2)), dma, dma, dma, dma, dma, dma,
        ],
        compiler_params=pltpu.CompilerParams(
            collective_id=0, has_side_effects=True, vmem_limit_bytes=56 * 2**20),
        cost_estimate=pl.CostEstimate(
            flops=4 * 32 * 1024 * 128 * 512, bytes_accessed=9 * 2**20, transcendentals=128),
    )(features[0, 0], adjacency[:, 0, 0], tile_mask[:, 0, 0].T, projection[0], row_gain)
    return out[None, None]


def solution(mesh):
    return jax.shard_map(
        shards,
        mesh=mesh,
        in_specs=(
            P("col", "row", None, None),
            P(None, "row", "col", None, None, None),
            P(None, "row", "col", None),
            P(),
            P(),
        ),
        out_specs=P("col", "row", None, None),
        check_vma=False,
    )
```

time: 61.2 us -> 67.2 us (1.098)
  Pallas kernels: 58.8 us -> 65.4 us
    pallas_call x1, Pallas kernels: 58.8 us -> 65.4 us  [shards(): pl.pallas_call(kernel, out_shape=jax.ShapeDtypeStruct((TILE, F), f32), in...]
where the time goes in v4:
time: 67.2 us; the launch traced here: 67.1 us
  Pallas kernels  65.4 us (97%)
  local copies, waits for them, and re-layouts  1.67 us (2%)
    pallas_call x1, Pallas kernels, shards(): pl.pallas_call(kernel, out_shape=jax.ShapeDtypeStruct((TILE, F), f32), in...  65.4 us
    unnamed x1, local copies, waits for them, and re-layouts  1.67 us

profile of v4, /device:TPU:1, one launch (start us, length us, event | category | flops | bytes accessed | tf_op | source)
XLA Modules:
  0.0 67.1 jit_solution(3700846220224166306)
XLA Ops:
  0.0 65.4 %shard_map.55 = f32[128,512]{1,0:T(8,128)} custom-call(f32[128,512]{1,0:T(8,128)} %bitcast.10, bf16[32,8,128,128]{3,2,1,0:T(8,128)(2,1)} %bitcast.8, s32[8,32]{1,0:T(8,128)} %bitcast.11, f32[512,512]{1,0:T(8,128)} %bitcast.9, f32[1,512]{1,0:T(1,128)} %g_ref.1), custom_call_target="tpu_custom_call" | custom-call | flops 8589934592 | bytes 9437184 | tf_op jit(solution)/shard_map/pallas_call | solution.py:357
  65.4 1.7 %copy.7 = f32[1,1,128,512]{3,2,1,0:T(8,128)} copy(f32[1,1,128,512]{3,2,1,0:T(8,128)} %bitcast.7) | data formatting | bytes 524288

commit v5 on v4

--- a/solution.py
+++ b/solution.py
@@ -13,8 +13,8 @@
 
 
 def kernel(x_ref, a_hbm, mask_ref, p_ref, g_ref, o_ref,
-           am, nat, ht, keep, snd, sib, cs0, cr0, cs1, cr1, xs, xr, hs, hr, acc, bs, br, ts, tr,
-           ns, nr, a_sem, row_s, row_r, xl_s, xl_r, agz_s, agz_r, hp_s, hp_r, xg_s, xg_r, sh_s, sh_r,
+           am, nat, ht, keep, snd, sib, cs0, cr0, cs1, cr1, xs, xr, hs, hr, acc, bs, br, ls, lr, ts, tr,
+           ns, nr, fs, lo_s, lo_r, a_sem, row_s, row_r, xl_s, xl_r, agz_s, agz_r, hp_s, hp_r, xg_s, xg_r, sh_s, sh_r,
            dd_s, dd_r, xx_s, xx_r, rsz_s, rsz_r, hx_s, hx_r, br_s, br_r, tt_s, tt_r,
            cg_s, cg_r, cn_s, cn_r):
     r = lax.axis_index("row")
@@ -58,8 +58,8 @@
         pltpu.make_async_copy(a_hbm.at[:, m], am.at[m], a_sem.at[m]).start()
 
     barrier = pltpu.get_barrier_semaphore()
-    peers = ([((r + j) % 8, c) for j in range(1, 8)]
-             + [sibling, hpartner, opposite, corner, *zdev, *zdiag])
+    peers = ([(row_at(j, 1), c) for j in range(1, 4)]
+             + [lpartner, sibling, hpartner, (r, block(0, 0, 1 - q)), *zdev, *zdiag])
     for dev in peers:
         pl.semaphore_signal(barrier, inc=1, device_id=dev, device_id_type=MESH)
 
@@ -153,12 +153,22 @@
     share(0, 1)
     corner_gather = remote(own, own, cg_s, cg_r, corner)
 
-    @pl.when(at_corner)
-    def _():
-        corner_gather.start()
+    def far_signal(i):
+        for dev in zdev:
+            pl.semaphore_signal(fs.at[i], inc=1, device_id=dev, device_id_type=MESH)
+
+    def far_wait(i):
+        pl.semaphore_wait(fs.at[i], 2)
+
+    far_signal(0)
     for m in range(5):
         mask_tiles(m)
+        if m % 2 == 1:
+            far_wait(m // 2)
+            far_signal(m // 2 + 1)
     ag_step(1, 0)
+    far_wait(2)
+    far_signal(3)
     mask_tiles(5)
     mask_tiles(6)
     x_lo_copy(False).wait_recv()
@@ -167,6 +177,11 @@
     start(remote(own, own, hp_s, hp_r, hpartner))
     ag_step(1, 1)
     mask_tiles(7)
+    far_wait(3)
+
+    @pl.when(at_corner)
+    def _():
+        corner_gather.start()
     ts[...] = am[r, opposite[1]]
     tile_copy = remote(ts, tr, tt_s, tt_r, opposite)
     start(tile_copy)
@@ -251,15 +266,15 @@
                 sums(slice(HALF, F), xr[d, rows])
             start(rsz(dirn, s, p))
 
-    def brow(j, same, sending=True):
-        dev = (row_at(j if sending else -j, same), c)
-        return remote(bs.at[j, same], br.at[j, same], br_s.at[j, same], br_r.at[j, same], dev)
+    def brow(j, same):
+        return remote(bs.at[j, same], br.at[j, same], br_s.at[j, same], br_r.at[j, same],
+                      (row_at(j, 1), c))
 
     def backward(j):
         back_pass((j,), (2, 6, 3, 5, 4), False)
         for same in range(2):
             bs[j, same] = acc[j, :, TILE * same:TILE * (same + 1)].astype(jnp.bfloat16)
-            if j or not same:
+            if j:
                 start(brow(j, same))
 
     corner_sums = remote(ns, nr, cn_s, cn_r, corner)
@@ -306,17 +321,21 @@
     rs_step(4, 1)
     rs_step(4, 2)
 
-    back = acc[0, :, TILE:]
+    def back_sum(same):
+        value = acc[0, :, TILE * same:TILE * (same + 1)]
+        for j in (1, 3, 2):
+            brow(j, same).wait_recv()
+            value = value + br[j, same].astype(jnp.float32)
+        return value
+
+    ls[...] = back_sum(0).astype(jnp.bfloat16)
+    across = remote(ls, lr, lo_s, lo_r, lpartner)
+    start(across)
     tile_copy.wait_recv()
-    back = back + lax.dot_general(ht[opposite[1]], tr[...], (((1,), (1,)), ((), ())),
-                                  preferred_element_type=jnp.float32)
-    for j in (2, 1, 3, 0):
-        for same in range(2):
-            if j or not same:
-                brow(j, same, False).wait_recv()
-                back = back + br[j, same].astype(jnp.float32)
+    back = back_sum(1) + lax.dot_general(ht[opposite[1]], tr[...], (((1,), (1,)), ((), ())),
+                                         preferred_element_type=jnp.float32)
     dd(0, 1).wait_recv()
-    keep[0, 1] = keep[0, 1] + sib[0, 1] + back.T
+    keep[0, 1] = keep[0, 1] + sib[0, 1]
 
     @pl.when(at_corner)
     def _():
@@ -329,6 +348,8 @@
                + cr0[1, 3].astype(jnp.float32)).astype(jnp.bfloat16)
     cross = remote(hs, hr, hx_s, hx_r, hpartner)
     start(cross)
+    across.wait_recv()
+    keep[0, 1] = keep[0, 1] + (back + lr[...].astype(jnp.float32)).T
     xx(0).wait_recv()
     for p in (1, 2):
         for dirn in range(2):
@@ -378,10 +399,13 @@
             pltpu.VMEM((4, F, 2 * TILE), f32),
             pltpu.VMEM((4, 2, F, TILE), bf),
             pltpu.VMEM((4, 2, F, TILE), bf),
+            pltpu.VMEM((F, TILE), bf),
+            pltpu.VMEM((F, TILE), bf),
             pltpu.VMEM((TILE, TILE), bf),
             pltpu.VMEM((TILE, TILE), bf),
             pltpu.VMEM((TILE, F), bf),
             pltpu.VMEM((TILE, F), bf),
+            pltpu.SemaphoreType.REGULAR((4,)), dma, dma,
             dma((NM,)), dma((4, 2)), dma((4, 2)), dma, dma, dma((2, 4, 3)), dma((2, 4, 3)),
             dma, dma, dma((8,)), dma((8,)), dma((8, 2)), dma((8, 2)),
             dma((8, 2)), dma((8, 2)), dma((8,)), dma((8,)), dma((2, 4, 3)), dma((2, 4, 3)),

time: 67.2 us -> 61.7 us (0.918)
  Pallas kernels: 65.4 us -> 59.9 us
    pallas_call x1, Pallas kernels: 65.4 us -> 59.9 us  [shards(): pl.pallas_call(kernel, out_shape=jax.ShapeDtypeStruct((TILE, F), f32), in...]
where the time goes in v5:
time: 61.7 us; the launch traced here: 61.6 us
  Pallas kernels  59.9 us (97%)
  local copies, waits for them, and re-layouts  1.67 us (3%)
    pallas_call x1, Pallas kernels, shards(): pl.pallas_call(kernel, out_shape=jax.ShapeDtypeStruct((TILE, F), f32), in...  59.9 us
    unnamed x1, local copies, waits for them, and re-layouts  1.67 us

profile of v5, /device:TPU:1, one launch (start us, length us, event | category | flops | bytes accessed | tf_op | source)
XLA Modules:
  0.0 61.6 jit_solution(1188522724045122627)
XLA Ops:
  0.0 59.9 %shard_map.55 = f32[128,512]{1,0:T(8,128)} custom-call(f32[128,512]{1,0:T(8,128)} %bitcast.10, bf16[32,8,128,128]{3,2,1,0:T(8,128)(2,1)} %bitcast.8, s32[8,32]{1,0:T(8,128)} %bitcast.11, f32[512,512]{1,0:T(8,128)} %bitcast.9, f32[1,512]{1,0:T(1,128)} %g_ref.1), custom_call_target="tpu_custom_call" | custom-call | flops 8589934592 | bytes 9437184 | tf_op jit(solution)/shard_map/pallas_call | solution.py:378
  59.9 1.7 %copy.7 = f32[1,1,128,512]{3,2,1,0:T(8,128)} copy(f32[1,1,128,512]{3,2,1,0:T(8,128)} %bitcast.7) | data formatting | bytes 524288

commit v6 on v5

--- a/solution.py
+++ b/solution.py
@@ -287,14 +287,14 @@
             corner_sums.start()
 
     forward((3, 5))
-    back_pass((3, 0), (1, 7), False)
+    ag_step(3, 2)
     forward((2, 6))
-    ag_step(3, 2)
-    for p in range(2):
-        ag_step(4, p)
     cross_sums(3)
     cross_sums(5)
     rs_step(2, 0)
+    for p in range(2):
+        ag_step(4, p)
+    back_pass((3, 0), (1, 7), False)
     forward((1, 7))
     corner_product()
     share_wait(2, 6, 3, 5)

time: 61.7 us -> 61.1 us (level)
  no operation moved by 1% of the time
where the time goes in v6:
time: 61.1 us; the launch traced here: 61 us
  Pallas kernels  59.3 us (97%)
  local copies, waits for them, and re-layouts  1.67 us (3%)
    pallas_call x1, Pallas kernels, shards(): pl.pallas_call(kernel, out_shape=jax.ShapeDtypeStruct((TILE, F), f32), in...  59.3 us
    unnamed x1, local copies, waits for them, and re-layouts  1.67 us

profile of v6, /device:TPU:1, one launch (start us, length us, event | category | flops | bytes accessed | tf_op | source)
XLA Modules:
  0.0 61.0 jit_solution(4664448146918917213)
XLA Ops:
  0.0 59.3 %shard_map.55 = f32[128,512]{1,0:T(8,128)} custom-call(f32[128,512]{1,0:T(8,128)} %bitcast.10, bf16[32,8,128,128]{3,2,1,0:T(8,128)(2,1)} %bitcast.8, s32[8,32]{1,0:T(8,128)} %bitcast.11, f32[512,512]{1,0:T(8,128)} %bitcast.9, f32[1,512]{1,0:T(1,128)} %g_ref.1), custom_call_target="tpu_custom_call" | custom-call | flops 8589934592 | bytes 9437184 | tf_op jit(solution)/shard_map/pallas_call | solution.py:378
  59.3 1.7 %copy.7 = f32[1,1,128,512]{3,2,1,0:T(8,128)} copy(f32[1,1,128,512]{3,2,1,0:T(8,128)} %bitcast.7) | data formatting | bytes 524288
